TPU v7x, 1024 devices: a whole 4x4x32 slice. The times are simulated.
1024 devices in a mesh: fsdp: 128 (over z, y), tp: 8 (over x, core).
Axes of the slice: x: 4, y: 4, z: 32, core: 2. Of those that a mesh axis runs over, the one named last changes fastest.
Arguments:
- trained_units: bfloat16 [8, 128, 128, 128], P('tp', 'fsdp'), may hold values from -0.046875 to 0.046875
- unit_place: int32 [8, 128], P('tp'), may hold values from 0 to 127, each once within a row
- hidden_states: bfloat16 [4, 128, 16384], P(None, 'fsdp', 'tp'), may hold values from -6 to 6
- probes: bfloat16 [512, 16384], P(None, 'tp'), may hold values from -6 to 6
- queries: bfloat16 [4, 128, 128, 128], P(None, 'fsdp', 'tp'), may hold values from -30 to 30
- key_cache: bfloat16 [128, 8, 2048, 128], P('fsdp', 'tp'), may hold values from -6 to 6
- value_cache: bfloat16 [128, 8, 2048, 128], P('fsdp', 'tp'), may hold values from -6 to 6
- new_values: bfloat16 [4, 128, 8, 128], P(None, 'fsdp', 'tp'), may hold values from -6 to 6
- cache_lengths: int32 [128], P('fsdp'), may hold values from 2 to 2044, as said below
Outputs:
- new_keys: bfloat16 [4, 128, 8, 128], P(None, 'fsdp', 'tp')
- attended: bfloat16 [4, 128, 128, 128], P(None, 'fsdp', 'tp')
- checksum: float32 [512, 1024], P(None, 'tp')
Inputs may be any that keep to these rules, and one draw needn't show every extreme that they name: Each row of unit_place names every block of its slab once. `cache_lengths`: some sequence has exactly 2044 live positions.
All inputs are finite; a program needn't handle non-finite values.
Results may differ from a plain program's by a relative error of at most 0.0051.
Values may be sent and summed in bfloat16 or wider, within the bound.
No kernel may reach another device: no remote copies, remote signals or barrier semaphores. Data moves between devices by JAX's collectives and lax.ppermute only.
A program may use at most 32 MiB of HBM per device.

v0:
```python
import jax
import jax.numpy as jnp
from jax import lax
from jax.sharding import PartitionSpec as P

ROPE_BASE = 500000.0


def rotate(vectors, positions):
    half_size = vectors.shape[-1] // 2
    frequency = ROPE_BASE ** (-jnp.arange(half_size, dtype=jnp.float32) * 2.0 / vectors.shape[-1])
    angles = positions.astype(jnp.float32)[..., None] * frequency
    cosine = jnp.cos(angles)
    sine_wave = jnp.sin(angles)
    first_half = vectors[..., :half_size]
    second_half = vectors[..., half_size:]
    return jnp.concatenate(
        [
            first_half * cosine - second_half * sine_wave,
            second_half * cosine + first_half * sine_wave,
        ],
        axis=-1,
    )


def slab_product(stacked, gathered, placement):
    slot_total = placement.shape[0]
    block_count = stacked.shape[1]
    head_count = slot_total // block_count
    head_size = gathered.shape[-1]
    slot_of = (
        jnp.zeros((slot_total,), jnp.int32)
        .at[placement]
        .set(jnp.arange(slot_total, dtype=jnp.int32))
    )
    ordered = jnp.take(gathered, slot_of, axis=0).reshape(
        block_count, head_count, head_size, head_size
    )
    return jnp.einsum("rbi,bhic->rhc", stacked, ordered, preferred_element_type=jnp.float32)


def on_device(
    trained_units,
    unit_place,
    hidden_states,
    probes,
    queries,
    key_cache,
    value_cache,
    new_values,
    cache_lengths,
):
    step_count, seq_count, slab_rows = hidden_states.shape
    head_size = trained_units.shape[-1]
    kv_local = key_cache.shape[1]
    group_size = queries.shape[2] // kv_local
    cache_len = key_cache.shape[2]
    key_rows = step_count * seq_count
    placement = unit_place[0]
    stacked = jnp.concatenate([hidden_states.reshape(key_rows, slab_rows), probes], axis=0)
    stacked = stacked.reshape(-1, slab_rows // head_size, head_size)
    gathered = lax.all_gather(trained_units, "fsdp", axis=1, tiled=True)[0]
    partial_value = slab_product(stacked, gathered, placement)[None]
    summed = lax.psum_scatter(partial_value, "tp", scatter_dimension=2, tiled=True)[0]
    raw_keys = summed[:key_rows].reshape(step_count, seq_count, kv_local, head_size)
    check_part = summed[key_rows:]
    checksum = check_part.reshape(check_part.shape[0], kv_local * head_size)
    positions = cache_lengths[None, :] + jnp.arange(step_count, dtype=jnp.int32)[:, None]
    new_keys = rotate(raw_keys, positions[:, :, None]).astype(jnp.bfloat16)
    score_scale = head_size ** (-0.5)
    queried = queries.reshape(step_count, seq_count, kv_local, group_size, head_size).transpose(
        1, 2, 0, 3, 4
    )
    queried = queried.reshape(seq_count, kv_local, step_count * group_size, head_size)
    fresh_keys = new_keys.transpose(1, 2, 0, 3)
    fresh_values = new_values.transpose(1, 2, 0, 3)
    fresh_scores = (
        jnp.einsum("rgmd,rgsd->rgms", queried, fresh_keys, preferred_element_type=jnp.float32)
        * score_scale
    )
    step_of = jnp.arange(step_count * group_size, dtype=jnp.int32) // group_size
    fresh_steps = jnp.arange(step_count, dtype=jnp.int32)
    fresh_scores = jnp.where(
        fresh_steps[None, None, None, :] <= step_of[None, None, :, None], fresh_scores, -jnp.inf
    )
    live_limit = cache_lengths[:, None, None, None]
    cache_scores = (
        jnp.einsum("rgmd,rgpd->rgmp", queried, key_cache, preferred_element_type=jnp.float32)
        * score_scale
    )
    cache_spots = jnp.arange(cache_len, dtype=jnp.int32)
    cache_scores = jnp.where(cache_spots[None, None, None, :] < live_limit, cache_scores, -jnp.inf)
    row_max = jnp.maximum(jnp.max(cache_scores, axis=-1), jnp.max(fresh_scores, axis=-1))[..., None]
    cache_exp = jnp.exp(cache_scores - row_max)
    fresh_exp = jnp.exp(fresh_scores - row_max)
    row_total = jnp.sum(cache_exp, axis=-1, keepdims=True) + jnp.sum(
        fresh_exp, axis=-1, keepdims=True
    )
    cache_weights = (cache_exp / row_total).astype(jnp.bfloat16)
    fresh_weights = (fresh_exp / row_total).astype(jnp.bfloat16)
    mixed_out = jnp.einsum(
        "rgmp,rgpd->rgmd", cache_weights, value_cache, preferred_element_type=jnp.float32
    )
    mixed_out = mixed_out + jnp.einsum(
        "rgms,rgsd->rgmd", fresh_weights, fresh_values, preferred_element_type=jnp.float32
    )
    attended = mixed_out.reshape(seq_count, kv_local, step_count, group_size, head_size).transpose(
        2, 0, 1, 3, 4
    )
    attended = attended.reshape(step_count, seq_count, kv_local * group_size, head_size).astype(
        jnp.bfloat16
    )
    return (new_keys, attended, checksum)


def solution(mesh):
    return jax.shard_map(
        on_device,
        mesh=mesh,
        in_specs=(
            P("tp", "fsdp", None, None),
            P("tp", None),
            P(None, "fsdp", "tp"),
            P(None, "tp"),
            P(None, "fsdp", "tp", None),
            P("fsdp", "tp", None, None),
            P("fsdp", "tp", None, None),
            P(None, "fsdp", "tp", None),
            P("fsdp"),
        ),
        out_specs=(P(None, "fsdp", "tp", None), P(None, "fsdp", "tp", None), P(None, "tp")),
        check_vma=False,
    )
```

profile of v0, /device:TPU:7, one launch (start us, length us, event | category | flops | bytes accessed | tf_op | source)
XLA Modules:
  0.0 411.5 jit_solution(18401736700451893368)
XLA Ops:
  7.2 0.0 copy-start
  7.2 0.0 all-gather.2.cloned.1.call-start
  7.2 0.7 all-gather.2.cloned.1.call-update
  7.9 0.0 all-reduce.3.cloned.1.call-start
  8.0 0.7 fusion.31
  8.6 1.0 scatter_custom_fusion
  9.6 0.1 broadcast_in_dim.46
  9.7 0.1 copy.22
  9.8 2.9 copy.20
  12.7 2.4 copy.21
  15.1 259.8 %all-gather.2.cloned.1.call-done = bf16[1,128,128,128]{3,2,0,1:T(8,128)(2,1)} async-done(((bf16[1,1,128,128]{3,2,0,1:T(8,128)(2,1)}), bf16[1,128,128,128]{3,2,0,1:T(8,128)(2,1)}) %all-gather.2.cloned.1.call-update) | async-done | bytes 4194320 | tf_op jit(solution)/shard_map/all_gather | solution.py:62
  274.9 0.0 copy-start.1
  274.9 0.0 copy-start.5
  274.9 5.4 %gather_fusion = bf16[128,128,128]{2,1,0:T(8,128)(2,1)} fusion(bf16[128,128,128]{2,1,0:T(8,128)(2,1)} %bitcast.48, s32[1024]{0:T(1024)S(1)} %pad_clamp_fusion), kind=kCustom, calls=%fused_computation | custom fusion | bytes 8389120 | tf_op jit(solution)/shard_map/jit(_take)/gather | solution.py:36
  280.3 0.0 copy-done.1
  280.3 0.0 copy-done.5
  280.3 4.4 %fusion.6 = f32[1,516,8,128]{3,1,2,0:T(8,128)S(1)} fusion(bf16[16,8,128,128]{3,2,1,0:T(8,128)(2,1)} %bitcast.49, pred[16,8]{0,1:T(8,128)(4,1)S(1)} %copy.22, bf16[512,16,128]{2,0,1:T(8,128)(2,1)S(1)} %copy-done.1, bf16[4,16,128]{2,0,1:T(4,128)(2,1)S(1)} %bitcast.58), kind=kOutput, calls=%fused_computation.11 | convolution fusion | flops 2170585088 | bytes 8421504 | tf_op jit(solution)/shard_map/rbi,bhic->rhc/dot_general | solution.py:39
  284.8 3.5 copy.25
  288.3 0.0 copy-start.2
  288.3 0.0 copy-start.4
  288.3 0.0 all-reduce.3.cloned.1.call-update
  288.3 0.0 copy-start.3
  289.0 1.4 dynamic-slice
  290.4 0.0 copy-done
  290.4 0.0 copy-done.2
  290.4 0.4 fusion.37
  290.8 107.7 %all-reduce.3.cloned.1.call-done = f32[1,516,8,128]{3,0,1,2:T(1,128)} async-done(((f32[1,516,8,128]{3,0,1,2:T(1,128)}), f32[1,516,8,128]{3,0,1,2:T(1,128)}) %all-reduce.3.cloned.1.call-update) | async-done | bytes 2113552
  398.6 1.4 constant_dynamic-slice_fusion
  399.9 0.1 fusion.21
  400.0 0.6 pad_maximum_fusion
  400.7 0.2 fusion.38
  400.9 0.3 fusion.13
  401.2 0.0 copy-done.4
  401.2 0.3 fusion.10
  401.5 0.0 copy-done.3
  401.5 0.8 fusion.7
  402.3 2.4 constant_dynamic-slice_fusion.1
  (11 shorter events, 0.1 us)
Async XLA Ops:
  7.2 283.2 %copy-start = (bf16[1,1,2048,128]{3,2,1,0:T(8,128)(2,1)S(1)}, bf16[1,1,2048,128]{3,2,1,0:T(8,128)(2,1)}, u32[]{:S(2)}) copy-start(bf16[1,1,2048,128]{3,2,1,0:T(8,128)(2,1)} %param.14) | copy-start | bytes 1572868
  7.2 267.8 %all-gather.2.cloned.1.call-start = ((), (), s32[]{:S(2)}) async-start(), calls=%async_computation | async-start | bytes 4227072 | tf_op jit(solution)/shard_map/all_gather | solution.py:62
  7.9 390.6 %all-reduce.3.cloned.1.call-start = ((), (), s32[]{:S(2)}) async-start(), calls=%async_computation.1 | async-start | bytes 4227072
  274.9 5.4 %copy-start.1 = (bf16[512,16,128]{2,0,1:T(8,128)(2,1)S(1)}, bf16[512,16,128]{2,0,1:T(8,128)(2,1)}, u32[]{:S(2)}) copy-start(bf16[512,16,128]{2,0,1:T(8,128)(2,1)} %copy.21) | copy-start | bytes 6291460
  274.9 5.4 %copy-start.5 = (bf16[4,1,2048]{2,0,1:T(4,128)(2,1)S(1)}, bf16[4,1,2048]{2,0,1:T(4,128)(2,1)}, u32[]{:S(2)}) copy-start(bf16[4,1,2048]{2,0,1:T(4,128)(2,1)} %param.11) | copy-start | bytes 49156
  288.3 2.1 copy-start.2
  288.3 112.9 %copy-start.4 = (bf16[1,1,2048,128]{3,2,1,0:T(8,128)(2,1)S(1)}, bf16[1,1,2048,128]{3,2,1,0:T(8,128)(2,1)}, u32[]{:S(2)}) copy-start(bf16[1,1,2048,128]{3,2,1,0:T(8,128)(2,1)} %param.15) | copy-start | bytes 1572868
  288.3 113.2 %copy-start.3 = (bf16[4,1,1,128]{3,0,2,1:T(4,128)(2,1)S(1)}, bf16[4,1,1,128]{3,0,2,1:T(4,128)(2,1)}, u32[]{:S(2)}) copy-start(bf16[4,1,1,128]{3,0,2,1:T(4,128)(2,1)} %param.16) | copy-start | bytes 3076
Sparse Core Ops, SparseCore 0:
  12.1 262.7 all-gather.1
  288.4 110.0 all-reduce.2
where the time goes:
time: 412 us
  waiting for transfers between devices  368 us (89%)
  local copies, waits for them, and re-layouts  20.4 us (5%)
  between operations  14.9 us (4%)
  matrix products  6.13 us (1%)
    all_gather x1, waiting for transfers between devices, on_device(): gathered = lax.all_gather(trained_units, 'fsdp', axis=1, tiled=True)[0]  260 us
    unnamed x3, waiting for transfers between devices  108 us
  transfers between devices with their start and end apart: 2, of which 2 were waited for; matrix products, arithmetic and copies ran while one was open for 2% of the time, Pallas kernels for 0%

commit v1 on v0

v1 whole, which is shorter than its diff:
```python
import jax
import jax.numpy as jnp
from jax import lax
from jax.experimental import pallas as pl
from jax.experimental.pallas import tpu as pltpu
from jax.sharding import Mesh, PartitionSpec as P

ROPE_BASE = 500000.0
BF16 = jnp.bfloat16
F32 = jnp.float32

FAR, NEAR, Y, X, CORES = 8, 4, 4, 4, 2
HEADS = X * CORES
STEPS = 4
HD = 128
CHECK = 512
SHARE = CHECK // Y
SEQ_ROWS = NEAR * STEPS
GROUP_ROWS = Y * SEQ_ROWS
PACK = SHARE + 2 * SEQ_ROWS


def split_sum(value):
    high = value.astype(BF16)
    return high, (value - high.astype(F32)).astype(BF16)


def product_kernel(block_ref, head_ref, unit_ref, hidden_ref, probe_ref, out_ref, total_ref):
    step = pl.program_id(0)

    @pl.when(step == 0)
    def _():
        total_ref[...] = jnp.zeros_like(total_ref)

    head = head_ref[step]
    unit = unit_ref[0]
    total_ref[head, :GROUP_ROWS] += jnp.dot(hidden_ref[...], unit, preferred_element_type=F32)
    total_ref[head, GROUP_ROWS:] += jnp.dot(probe_ref[...], unit, preferred_element_type=F32)

    @pl.when(step == FAR - 1)
    def _():
        for y in range(Y):
            high, low = split_sum(total_ref[:, y * SEQ_ROWS : (y + 1) * SEQ_ROWS])
            out_ref[y, :, SHARE : SHARE + SEQ_ROWS] = high
            out_ref[y, :, SHARE + SEQ_ROWS :] = low
            start = GROUP_ROWS + y * SHARE
            out_ref[y, :, :SHARE] = total_ref[:, start : start + SHARE].astype(BF16)


def products(blocks, heads, units, hidden, probes):
    return pl.pallas_call(
        product_kernel,
        grid_spec=pltpu.PrefetchScalarGridSpec(
            num_scalar_prefetch=2,
            grid=(FAR,),
            in_specs=[
                pl.BlockSpec((1, HD, HD), lambda k, b, h: (k, 0, 0)),
                pl.BlockSpec((GROUP_ROWS, HD), lambda k, b, h: (0, b[k])),
                pl.BlockSpec((CHECK, HD), lambda k, b, h: (0, b[k])),
            ],
            out_specs=pl.BlockSpec((Y, HEADS, PACK, HD), lambda k, b, h: (0, 0, 0, 0)),
            scratch_shapes=[pltpu.VMEM((HEADS, GROUP_ROWS + CHECK, HD), F32)],
        ),
        out_shape=jax.ShapeDtypeStruct((Y, HEADS, PACK, HD), BF16),
        compiler_params=pltpu.CompilerParams(vmem_limit_bytes=24 << 20),
        cost_estimate=pl.CostEstimate(flops=2 * FAR * (GROUP_ROWS + CHECK) * HD * HD, bytes_accessed=4 << 20, transcendentals=0),
        name="products",
    )(blocks, heads, units, hidden, probes)


def cached_kernel(length_ref, query_ref, key_ref, value_ref, max_ref, total_ref, mixed_ref):
    scores = lax.dot_general(query_ref[...], key_ref[...], (((1,), (1,)), ((), ())), preferred_element_type=F32)
    spots = lax.broadcasted_iota(jnp.int32, scores.shape, 1)
    scores = jnp.where(spots < length_ref[0], scores * HD**-0.5, -jnp.inf)
    largest = jnp.max(scores, axis=1, keepdims=True)
    weights = jnp.exp(scores - largest)
    high, low = split_sum(weights)
    values = value_ref[...]
    mixed_ref[...] = jnp.dot(high, values, preferred_element_type=F32) + jnp.dot(low, values, preferred_element_type=F32)
    max_ref[...] = jnp.broadcast_to(largest, max_ref.shape)
    total_ref[...] = jnp.broadcast_to(jnp.sum(weights, axis=1, keepdims=True), total_ref.shape)


def cached_attention(lengths, queries, keys, values):
    rows, spots = queries.shape[0], keys.shape[0]
    vmem = pl.BlockSpec(memory_space=pltpu.VMEM)
    shape = jax.ShapeDtypeStruct((rows, HD), F32)
    return pl.pallas_call(
        cached_kernel,
        in_specs=[pl.BlockSpec(memory_space=pltpu.SMEM), vmem, vmem, vmem],
        out_specs=[vmem] * 3,
        out_shape=[shape] * 3,
        compiler_params=pltpu.CompilerParams(vmem_limit_bytes=24 << 20),
        cost_estimate=pl.CostEstimate(flops=6 * rows * spots * HD, bytes_accessed=4 * spots * HD, transcendentals=rows * spots),
        name="cached_attention",
    )(lengths, queries, keys, values)


def fresh_kernel(raw_ref, cosine_ref, sine_ref, query_ref, value_ref, max_ref, total_ref, mixed_ref, key_ref, out_ref):
    raw = raw_ref[...]
    turned = raw * cosine_ref[...] + pltpu.roll(raw, HD // 2, 1) * sine_ref[...]
    new_keys = turned.astype(BF16)
    key_ref[...] = new_keys[:STEPS]
    scores = lax.dot_general(query_ref[...], new_keys, (((1,), (1,)), ((), ())), preferred_element_type=F32)
    rows = lax.broadcasted_iota(jnp.int32, scores.shape, 0)
    steps = lax.broadcasted_iota(jnp.int32, scores.shape, 1)
    group = query_ref.shape[0] // STEPS
    scores = jnp.where(steps * group <= rows, scores * HD**-0.5, -jnp.inf)
    cached_max = max_ref[:, :1]
    largest = jnp.maximum(cached_max, jnp.max(scores, axis=1, keepdims=True))
    keep = jnp.exp(cached_max - largest)
    weights = jnp.exp(scores - largest)
    total = total_ref[:, :1] * keep + jnp.sum(weights, axis=1, keepdims=True)
    values = value_ref[...].astype(F32)
    mixed = mixed_ref[...] * keep
    for s in range(STEPS):
        mixed += weights[:, s : s + 1] * values[s : s + 1]
    out_ref[...] = (mixed / total).astype(BF16)


def fresh_attention(raw, cosine, sine, queries, values, cached):
    vmem = pl.BlockSpec(memory_space=pltpu.VMEM)
    return pl.pallas_call(
        fresh_kernel,
        in_specs=[vmem] * 8,
        out_specs=[vmem] * 2,
        out_shape=[jax.ShapeDtypeStruct((STEPS, HD), BF16), jax.ShapeDtypeStruct(queries.shape, BF16)],
        cost_estimate=pl.CostEstimate(flops=1 << 18, bytes_accessed=1 << 17, transcendentals=1024),
        name="fresh_attention",
    )(raw, cosine, sine, queries, values, *cached)


def spread(value, axis, copies):
    return lax.all_to_all(jnp.broadcast_to(value[None], (copies, *value.shape)), axis, 0, 0, tiled=True)


def on_device(trained_units, unit_place, hidden_states, probes, queries, key_cache, value_cache, new_values, cache_lengths):
    mine = lax.axis_index("zl") * Y + lax.axis_index("y")
    places = lax.dynamic_index_in_dim(unit_place.reshape(FAR, NEAR * Y), mine, axis=1, keepdims=False)
    units = spread(trained_units[0, 0], "zh", FAR)
    hidden = lax.all_gather(hidden_states[:, 0], "zl", axis=0)
    hidden = lax.all_gather(hidden, "y", axis=0).reshape(GROUP_ROWS, -1)

    query_rows = queries.reshape(-1, HD)
    cached = cached_attention(cache_lengths, query_rows, key_cache[0, 0], value_cache[0, 0])
    frequency = ROPE_BASE ** (-jnp.arange(HD // 2, dtype=F32) * 2.0 / HD)
    positions = cache_lengths + jnp.arange(2 * STEPS, dtype=jnp.int32)
    angles = positions.astype(F32)[:, None] * frequency
    cosine, sine = jnp.cos(angles), jnp.sin(angles)
    cosine = jnp.concatenate([cosine, cosine], axis=1)
    sine = jnp.concatenate([-sine, sine], axis=1)

    packed = products(places // HEADS, places % HEADS, units, hidden, probes)
    packed = lax.all_to_all(packed.reshape(Y * HEADS, PACK, HD), ("y", "x", "c"), 0, 0, tiled=True)
    packed = jnp.sum(packed.astype(F32), axis=0)
    raw = packed[SHARE : SHARE + SEQ_ROWS] + packed[SHARE + SEQ_ROWS :]
    share = jnp.broadcast_to(packed[None, :SHARE].astype(BF16), (NEAR, SHARE, HD))
    high, low = split_sum(raw.reshape(NEAR, STEPS, HD))
    packed = jnp.concatenate([share, high, low, jnp.zeros((NEAR, 2 * STEPS, HD), BF16)], axis=1)
    packed = lax.all_to_all(packed, "zl", 0, 0, tiled=True)
    packed = jnp.sum(packed.astype(F32), axis=0)
    raw = packed[SHARE : SHARE + STEPS] + packed[SHARE + STEPS : SHARE + 2 * STEPS]
    raw = jnp.concatenate([raw, jnp.zeros_like(raw)], axis=0)
    checksum = spread(packed[:SHARE].astype(BF16), "y", Y).reshape(CHECK, HD).astype(F32)

    new_keys, attended = fresh_attention(raw, cosine, sine, query_rows, new_values.reshape(STEPS, HD), cached)
    return new_keys.reshape(STEPS, 1, 1, HD), attended.reshape(queries.shape), checksum


def solution(mesh):
    own = Mesh(mesh.devices.reshape(FAR, NEAR, Y, X, CORES), ("zh", "zl", "y", "x", "c"))
    fsdp, tp = ("zh", "zl", "y"), ("x", "c")
    return jax.shard_map(
        on_device,
        mesh=own,
        in_specs=(
            P(tp, fsdp, None, None),
            P(tp, None),
            P(None, fsdp, tp),
            P(None, tp),
            P(None, fsdp, tp, None),
            P(fsdp, tp, None, None),
            P(fsdp, tp, None, None),
            P(None, fsdp, tp, None),
            P(fsdp),
        ),
        out_specs=(P(None, fsdp, tp, None), P(None, fsdp, tp, None), P(None, tp)),
        check_vma=False,
    )
```

time: 412 us -> 127 us (0.31)
  the two profiles are of different devices: /device:TPU:7 before, /device:TPU:256 now
where the time goes in v1:
time: 127 us
  blocking collectives  41.3 us (33%)
  starting transfers between devices  40.6 us (32%)
  waiting for transfers between devices  25.9 us (20%)
  Pallas kernels  6.7 us (5%)
  local copies, waits for them, and re-layouts  6.49 us (5%)
  other arithmetic  4.2 us (3%)
  between operations  1.47 us (1%)
    all_to_all x2, starting transfers between devices, spread(): lax.all_to_all(jnp.broadcast_to(value[None], (copies, *value.shape)), axi...  28.6 us
    all_gather x1, blocking collectives, on_device(): hidden = lax.all_gather(hidden_states[:, 0], 'zl', axis=0)  28.5 us
    all_to_all x1, waiting for transfers between devices, on_device(): lax.all_to_all(packed.reshape(Y * HEADS, PACK, HD), ('y', 'x', 'c'), 0, 0...  20.7 us
    all_gather x1, blocking collectives, on_device(): hidden = lax.all_gather(hidden, 'y', axis=0).reshape(GROUP_ROWS, -1)  12.8 us
    all_to_all x1, starting transfers between devices, on_device(): lax.all_to_all(packed.reshape(Y * HEADS, PACK, HD), ('y', 'x', 'c'), 0, 0...  6.77 us
    all_to_all x1, starting transfers between devices, on_device(): packed = lax.all_to_all(packed, 'zl', 0, 0, tiled=True)  5.2 us
    pallas_call x1, Pallas kernels, products(): pl.pallas_call(product_kernel, grid_spec=pltpu.PrefetchScalarGridSpec(num...  3.93 us
    all_to_all x2, waiting for transfers between devices, spread(): lax.all_to_all(jnp.broadcast_to(value[None], (copies, *value.shape)), axi...  3.28 us
  transfers between devices with their start and end apart: 4, of which 3 were waited for; matrix products, arithmetic and copies ran while one was open for 4% of the time, Pallas kernels for 2%

profile of v1, /device:TPU:256, one launch (start us, length us, event | category | flops | bytes accessed | tf_op | source)
XLA Modules:
  0.0 126.5 jit_solution(5614268380948329650)
XLA Ops:
  0.6 0.0 copy-start
  0.6 1.6 %broadcast_in_dim.11 = bf16[8,128,128]{2,1,0:T(8,128)(2,1)} broadcast(bf16[128,128]{1,0:T(8,128)(2,1)} %bitcast.20), dimensions={1,2} | broadcast | bytes 294912 | tf_op jit(solution)/shard_map/broadcast_in_dim | solution.py:134
  2.3 25.3 %all-to-all-start = ((bf16[8,128,128]{2,1,0:T(8,128)(2,1)}), bf16[8,128,128]{2,1,0:T(8,128)(2,1)S(1)}, u32[]{:S(2)}, u32[]{:S(2)}) async-start(bf16[8,128,128]{2,1,0:T(8,128)(2,1)} %broadcast_in_dim.11), calls=%async_computation | async-start | bytes 524288 | tf_op jit(solution)/shard_map/all_to_all | solution.py:134
  27.5 0.5 broadcast.54
  28.1 1.3 %reduce.6 = s32[128]{0:T(128)S(1)} reduce(s32[1,128]{1,0:T(1,128)} %param.10, s32[]{:T(128)} %broadcast.54), dimensions={0}, to_apply=%param.10.reduce_sub_computation.3 | reduce | bytes 1028 | tf_op args[1]
  29.4 0.1 reshape.48
  29.5 0.7 copy.18
  30.2 28.5 %all-gather = bf16[16,1,2048]{2,1,0:T(2,128)(2,1)S(1)} all-gather(bf16[4,1,2048]{2,1,0:T(2,128)(2,1)S(1)} %copy.18), channel_id=2, replica_groups=mesh['zh'=8,'zl'=4,'y'=4,'x'=4,'c'=2] {'zl'}, dimensions={0}, use_global_device_ids=true | all-gather | bytes 81920 | tf_op jit(solution)/shard_map/all_gather | solution.py:141
  58.7 0.4 reduce.2
  59.1 12.8 %all-gather.1 = bf16[16,4,2048]{2,1,0:T(4,128)(2,1)S(1)} all-gather(bf16[4,4,2048]{2,1,0:T(4,128)(2,1)S(1)} %reshape.57), channel_id=3, replica_groups=mesh['zh'=8,'zl'=4,'y'=4,'x'=4,'c'=2] {'y'}, dimensions={0}, use_global_device_ids=true | all-gather | bytes 327680 | tf_op jit(solution)/shard_map/all_gather | solution.py:142
  71.9 0.1 reshape.49.hidden_ref
  71.9 0.2 dynamic-slice_reduce_fusion
  72.1 0.0 all-to-all-done.unit_ref
  72.1 0.0 copy-done
  72.1 3.9 %products.1 = bf16[4,8,160,128]{3,2,1,0:T(8,128)(2,1)} custom-call(s32[8]{0:T(128)S(1)} %get-tuple-element.34.block_ref, s32[8]{0:T(128)S(1)} %get-tuple-element.33.head_ref, bf16[8,128,128]{2,1,0:T(8,128)(2,1)S(1)} %all-to-all-done.unit_ref, bf16[64,2048]{1,0:T(8,128)(2,1)S(1)} %reshape.49.hidden_ref, bf16[512,2048]{1,0:T(8,128)(2,1)S(1)} %copy-done), custom_call_target="tpu_custom_call" | custom-call | flops 150994944 | bytes 4194304 | tf_op jit(solution)/shard_map/products/pallas_call | solution.py:51
  76.1 6.8 %all-to-all-start.1 = ((bf16[32,160,128]{2,1,0:T(8,128)(2,1)}), bf16[32,160,128]{2,1,0:T(8,128)(2,1)S(1)}, u32[]{:S(2)}, u32[]{:S(2)}) async-start(bf16[32,160,128]{2,1,0:T(8,128)(2,1)} %bitcast.1), calls=%async_computation.1 | async-start | bytes 2621440 | tf_op jit(solution)/shard_map/all_to_all | solution.py:154
  82.9 0.0 copy-start.1
  82.9 0.0 copy-start.2
  82.9 0.0 copy-start.3
  82.9 0.1 pad.8.clone
  83.0 20.7 %all-to-all-done.1 = bf16[32,160,128]{2,1,0:T(8,128)(2,1)S(1)} async-done(((bf16[32,160,128]{2,1,0:T(8,128)(2,1)}), bf16[32,160,128]{2,1,0:T(8,128)(2,1)S(1)}, u32[]{:S(2)}, u32[]{:S(2)}) %all-to-all-start.1) | async-done | bytes 1310752 | tf_op jit(solution)/shard_map/all_to_all | solution.py:154
  103.6 0.2 convert_reduce_fusion
  103.9 0.8 maximum_maximum_fusion
  104.7 5.2 %all-to-all-start.2 = ((bf16[4,144,128]{2,1,0:T(8,128)(2,1)}), bf16[4,144,128]{2,1,0:T(8,128)(2,1)S(1)}, u32[]{:S(2)}, u32[]{:S(2)}) async-start(bf16[4,144,128]{2,1,0:T(8,128)(2,1)} %maximum_maximum_fusion), calls=%async_computation.2 | async-start | bytes 294912 | tf_op jit(solution)/shard_map/all_to_all | solution.py:160
  110.5 0.0 copy-done.1
  110.5 0.0 copy-done.2
  110.5 0.0 copy-done.3
  110.5 0.7 cached_attention.1
  111.3 0.0 copy-start.4
  111.3 0.6 copy-done.4
  111.9 0.0 copy-start.5
  111.9 0.6 copy-done.5
  112.5 0.0 copy-start.6
  112.5 0.6 copy-done.6
  113.1 0.1 fusion
  113.2 0.7 pad_maximum_fusion
  113.9 1.9 %all-to-all-done.2 = bf16[4,144,128]{2,1,0:T(8,128)(2,1)S(1)} async-done(((bf16[4,144,128]{2,1,0:T(8,128)(2,1)}), bf16[4,144,128]{2,1,0:T(8,128)(2,1)S(1)}, u32[]{:S(2)}, u32[]{:S(2)}) %all-to-all-start.2) | async-done | bytes 147488 | tf_op jit(solution)/shard_map/all_to_all | solution.py:160
  115.9 0.7 broadcast_in_dim.14
  116.5 3.3 %all-to-all-start.3 = ((bf16[4,128,128]{2,1,0:T(8,128)(2,1)}), bf16[4,128,128]{2,1,0:T(8,128)(2,1)S(1)}, u32[]{:S(2)}, u32[]{:S(2)}) async-start(bf16[4,128,128]{2,1,0:T(8,128)(2,1)} %broadcast_in_dim.14), calls=%async_computation.3 | async-start | bytes 262144 | tf_op jit(solution)/shard_map/all_to_all | solution.py:134
  119.9 0.6 concatenate.13.raw_ref
  120.5 2.1 %fresh_attention.1 = (bf16[4,128]{1,0:T(4,128)(2,1)}, bf16[64,128]{1,0:T(8,128)(2,1)}) custom-call(f32[8,128]{1,0:T(8,128)} %concatenate.13.raw_ref, f32[8,128]{1,0:T(8,128)} %get-tuple-element.35.cosine_ref, f32[8,128]{1,0:T(8,128)} %get-tuple-element.36.sine_ref, bf16[64,128]{1,0:T(8,128)(2,1)} %bitcast.18, bf16[4,128]{1,0:T(4,128)(2,1)} %bitcast.22, ...), custom_call_target="tpu_custom_call" | custom-call | flops 262144 | bytes 131072 | tf_op jit(solution)/shard_map/fresh_attention/pallas_call | solution.py:123
  122.5 3.3 %all-to-all-done.3 = bf16[4,128,128]{2,1,0:T(8,128)(2,1)S(1)} async-done(((bf16[4,128,128]{2,1,0:T(8,128)(2,1)}), bf16[4,128,128]{2,1,0:T(8,128)(2,1)S(1)}, u32[]{:S(2)}, u32[]{:S(2)}) %all-to-all-start.3) | async-done | bytes 131104 | tf_op jit(solution)/shard_map/all_to_all | solution.py:134
  125.8 0.7 bitcast_convert_fusion
  (12 shorter events, 0.1 us)
Async XLA Ops:
  0.6 71.5 %copy-start = (bf16[512,2048]{1,0:T(8,128)(2,1)S(1)}, bf16[512,2048]{1,0:T(8,128)(2,1)}, u32[]{:S(2)}) copy-start(bf16[512,2048]{1,0:T(8,128)(2,1)} %probe_ref.1) | copy-start | bytes 6291460
  2.3 69.8 %all-to-all-start = ((bf16[8,128,128]{2,1,0:T(8,128)(2,1)}), bf16[8,128,128]{2,1,0:T(8,128)(2,1)S(1)}, u32[]{:S(2)}, u32[]{:S(2)}) async-start(bf16[8,128,128]{2,1,0:T(8,128)(2,1)} %broadcast_in_dim.11), calls=%async_computation | async-start | bytes 524288 | tf_op jit(solution)/shard_map/all_to_all | solution.py:134
  76.1 27.6 %all-to-all-start.1 = ((bf16[32,160,128]{2,1,0:T(8,128)(2,1)}), bf16[32,160,128]{2,1,0:T(8,128)(2,1)S(1)}, u32[]{:S(2)}, u32[]{:S(2)}) async-start(bf16[32,160,128]{2,1,0:T(8,128)(2,1)} %bitcast.1), calls=%async_computation.1 | async-start | bytes 2621440 | tf_op jit(solution)/shard_map/all_to_all | solution.py:154
  82.9 27.7 %copy-start.1 = (bf16[1,1,2048,128]{3,2,1,0:T(8,128)(2,1)S(1)}, bf16[1,1,2048,128]{3,2,1,0:T(8,128)(2,1)}, u32[]{:S(2)}) copy-start(bf16[1,1,2048,128]{3,2,1,0:T(8,128)(2,1)} %param.14) | copy-start | bytes 1572868
  82.9 27.7 %copy-start.2 = (bf16[1,1,2048,128]{3,2,1,0:T(8,128)(2,1)S(1)}, bf16[1,1,2048,128]{3,2,1,0:T(8,128)(2,1)}, u32[]{:S(2)}) copy-start(bf16[1,1,2048,128]{3,2,1,0:T(8,128)(2,1)} %param.15) | copy-start | bytes 1572868
  82.9 27.7 %copy-start.3 = (bf16[4,1,16,128]{3,2,1,0:T(8,128)(2,1)S(1)}, bf16[4,1,16,128]{3,2,1,0:T(8,128)(2,1)}, u32[]{:S(2)}) copy-start(bf16[4,1,16,128]{3,2,1,0:T(8,128)(2,1)} %param.13) | copy-start | bytes 49156
  104.7 11.2 %all-to-all-start.2 = ((bf16[4,144,128]{2,1,0:T(8,128)(2,1)}), bf16[4,144,128]{2,1,0:T(8,128)(2,1)S(1)}, u32[]{:S(2)}, u32[]{:S(2)}) async-start(bf16[4,144,128]{2,1,0:T(8,128)(2,1)} %maximum_maximum_fusion), calls=%async_computation.2 | async-start | bytes 294912 | tf_op jit(solution)/shard_map/all_to_all | solution.py:160
  111.3 0.6 copy-start.4
  111.9 0.6 copy-start.5
  112.5 0.6 copy-start.6
  116.5 9.3 %all-to-all-start.3 = ((bf16[4,128,128]{2,1,0:T(8,128)(2,1)}), bf16[4,128,128]{2,1,0:T(8,128)(2,1)S(1)}, u32[]{:S(2)}, u32[]{:S(2)}) async-start(bf16[4,128,128]{2,1,0:T(8,128)(2,1)} %broadcast_in_dim.14), calls=%async_computation.3 | async-start | bytes 262144 | tf_op jit(solution)/shard_map/all_to_all | solution.py:134

commit v2 on v1

--- a/solution.py
+++ b/solution.py
@@ -40,7 +40,8 @@
     @pl.when(step == FAR - 1)
     def _():
         for y in range(Y):
-            high, low = split_sum(total_ref[:, y * SEQ_ROWS : (y + 1) * SEQ_ROWS])
+            starts = [(plane * Y + y) * STEPS for plane in range(NEAR)]
+            high, low = split_sum(jnp.concatenate([total_ref[:, start : start + STEPS] for start in starts], axis=1))
             out_ref[y, :, SHARE : SHARE + SEQ_ROWS] = high
             out_ref[y, :, SHARE + SEQ_ROWS :] = low
             start = GROUP_ROWS + y * SHARE
@@ -138,8 +139,8 @@
     mine = lax.axis_index("zl") * Y + lax.axis_index("y")
     places = lax.dynamic_index_in_dim(unit_place.reshape(FAR, NEAR * Y), mine, axis=1, keepdims=False)
     units = spread(trained_units[0, 0], "zh", FAR)
-    hidden = lax.all_gather(hidden_states[:, 0], "zl", axis=0)
-    hidden = lax.all_gather(hidden, "y", axis=0).reshape(GROUP_ROWS, -1)
+    hidden = lax.all_gather(hidden_states[:, 0], "y", axis=0).reshape(Y * STEPS, -1)
+    hidden = lax.all_gather(hidden, "zl", axis=0).reshape(GROUP_ROWS, -1)
 
     query_rows = queries.reshape(-1, HD)
     cached = cached_attention(cache_lengths, query_rows, key_cache[0, 0], value_cache[0, 0])

time: 127 us -> 127 us (level)
  the two profiles are of different devices: /device:TPU:256 before, /device:TPU:32 now
where the time goes in v2:
time: 127 us
  starting transfers between devices  41.3 us (33%)
  waiting for transfers between devices  34.5 us (27%)
  blocking collectives  30.9 us (24%)
  local copies, waits for them, and re-layouts  7.86 us (6%)
  Pallas kernels  6.71 us (5%)
  other arithmetic  3.84 us (3%)
  between operations  1.44 us (1%)
    all_to_all x2, starting transfers between devices, spread(): lax.all_to_all(jnp.broadcast_to(value[None], (copies, *value.shape)), axi...  30.8 us
    all_to_all x1, waiting for transfers between devices, on_device(): lax.all_to_all(packed.reshape(Y * HEADS, PACK, HD), ('y', 'x', 'c'), 0, 0...  20.7 us
    all_gather x1, blocking collectives, on_device(): hidden = lax.all_gather(hidden, 'zl', axis=0).reshape(GROUP_ROWS, -1)  18.4 us
    all_to_all x2, waiting for transfers between devices, spread(): lax.all_to_all(jnp.broadcast_to(value[None], (copies, *value.shape)), axi...  12.6 us
    all_gather x1, blocking collectives, on_device(): lax.all_gather(hidden_states[:, 0], 'y', axis=0).reshape(Y * STEPS, -1)  12.5 us
    all_to_all x1, starting transfers between devices, on_device(): lax.all_to_all(packed.reshape(Y * HEADS, PACK, HD), ('y', 'x', 'c'), 0, 0...  7.16 us
    unnamed x16, local copies, waits for them, and re-layouts  4.67 us
    pallas_call x1, Pallas kernels, products(): pl.pallas_call(product_kernel, grid_spec=pltpu.PrefetchScalarGridSpec(num...  3.94 us
  transfers between devices with their start and end apart: 4, of which 4 were waited for; matrix products, arithmetic and copies ran while one was open for 3% of the time, Pallas kernels for 2%

profile of v2, /device:TPU:32, one launch (start us, length us, event | category | flops | bytes accessed | tf_op | source)
XLA Modules:
  0.0 126.6 jit_solution(14036303178068681153)
XLA Ops:
  0.6 1.5 %broadcast_in_dim.11 = bf16[8,128,128]{2,1,0:T(8,128)(2,1)} broadcast(bf16[128,128]{1,0:T(8,128)(2,1)} %bitcast.22), dimensions={1,2} | broadcast | bytes 294912 | tf_op jit(solution)/shard_map/broadcast_in_dim | solution.py:135
  2.1 27.4 %all-to-all-start = ((bf16[8,128,128]{2,1,0:T(8,128)(2,1)}), bf16[8,128,128]{2,1,0:T(8,128)(2,1)S(1)}, u32[]{:S(2)}, u32[]{:S(2)}) async-start(bf16[8,128,128]{2,1,0:T(8,128)(2,1)} %broadcast_in_dim.11), calls=%async_computation | async-start | bytes 524288 | tf_op jit(solution)/shard_map/all_to_all | solution.py:135
  29.6 0.5 broadcast.53
  30.1 1.3 %reduce.5 = s32[128]{0:T(128)S(1)} reduce(s32[1,128]{1,0:T(1,128)} %param.10, s32[]{:T(128)} %broadcast.53), dimensions={0}, to_apply=%param.10.reduce_sub_computation.3 | reduce | bytes 1028 | tf_op args[1]
  31.4 0.1 reshape.48
  31.5 0.7 copy.17
  32.2 12.5 %all-gather = bf16[16,1,2048]{2,1,0:T(2,128)(2,1)S(1)} all-gather(bf16[4,1,2048]{2,1,0:T(2,128)(2,1)S(1)} %copy.17), channel_id=2, replica_groups=mesh['zh'=8,'zl'=4,'y'=4,'x'=4,'c'=2] {'y'}, dimensions={0}, use_global_device_ids=true | all-gather | bytes 81920 | tf_op jit(solution)/shard_map/all_gather | solution.py:142
  44.8 0.2 dynamic-slice_reduce_fusion
  45.0 18.4 %all-gather.1 = bf16[64,1,2048]{2,0,1:T(8,128)(2,1)S(1)} all-gather(bf16[16,1,2048]{2,0,1:T(8,128)(2,1)S(1)} %copy.18), channel_id=3, replica_groups=mesh['zh'=8,'zl'=4,'y'=4,'x'=4,'c'=2] {'zl'}, dimensions={0}, use_global_device_ids=true | all-gather | bytes 327680 | tf_op jit(solution)/shard_map/all_gather | solution.py:143
  63.4 9.3 %all-to-all-done.unit_ref = bf16[8,128,128]{2,1,0:T(8,128)(2,1)S(1)} async-done(((bf16[8,128,128]{2,1,0:T(8,128)(2,1)}), bf16[8,128,128]{2,1,0:T(8,128)(2,1)S(1)}, u32[]{:S(2)}, u32[]{:S(2)}) %all-to-all-start) | async-done | bytes 262176 | tf_op jit(solution)/shard_map/all_to_all | solution.py:135
  72.7 0.0 copy-start
  72.7 1.6 %copy-done = bf16[512,2048]{1,0:T(8,128)(2,1)S(1)} copy-done((bf16[512,2048]{1,0:T(8,128)(2,1)S(1)}, bf16[512,2048]{1,0:T(8,128)(2,1)}, u32[]{:S(2)}) %copy-start) | copy-done | bytes 2097176
  74.3 3.9 %products.1 = bf16[4,8,160,128]{3,2,1,0:T(8,128)(2,1)} custom-call(s32[8]{0:T(128)S(1)} %get-tuple-element.31.block_ref, s32[8]{0:T(128)S(1)} %get-tuple-element.30.head_ref, bf16[8,128,128]{2,1,0:T(8,128)(2,1)S(1)} %all-to-all-done.unit_ref, bf16[64,2048]{1,0:T(8,128)(2,1)S(1)} %bitcast.17, bf16[512,2048]{1,0:T(8,128)(2,1)S(1)} %copy-done), custom_call_target="tpu_custom_call" | custom-call | flops 150994944 | bytes 4194304 | tf_op jit(solution)/shard_map/products/pallas_call | solution.py:52
  78.2 7.2 %all-to-all-start.1 = ((bf16[32,160,128]{2,1,0:T(8,128)(2,1)}), bf16[32,160,128]{2,1,0:T(8,128)(2,1)S(1)}, u32[]{:S(2)}, u32[]{:S(2)}) async-start(bf16[32,160,128]{2,1,0:T(8,128)(2,1)} %bitcast.2), calls=%async_computation.1 | async-start | bytes 2621440 | tf_op jit(solution)/shard_map/all_to_all | solution.py:155
  85.4 0.0 copy-start.1
  85.4 0.0 copy-start.2
  85.4 0.0 copy-start.3
  85.4 0.1 pad.8.clone
  85.5 20.7 %all-to-all-done.1 = bf16[32,160,128]{2,1,0:T(8,128)(2,1)S(1)} async-done(((bf16[32,160,128]{2,1,0:T(8,128)(2,1)}), bf16[32,160,128]{2,1,0:T(8,128)(2,1)S(1)}, u32[]{:S(2)}, u32[]{:S(2)}) %all-to-all-start.1) | async-done | bytes 1310752 | tf_op jit(solution)/shard_map/all_to_all | solution.py:155
  106.2 0.2 convert_reduce_fusion
  106.4 0.8 maximum_maximum_fusion
  107.2 3.4 %all-to-all-start.2 = ((bf16[4,144,128]{2,1,0:T(8,128)(2,1)}), bf16[4,144,128]{2,1,0:T(8,128)(2,1)S(1)}, u32[]{:S(2)}, u32[]{:S(2)}) async-start(bf16[4,144,128]{2,1,0:T(8,128)(2,1)} %maximum_maximum_fusion), calls=%async_computation.2 | async-start | bytes 294912 | tf_op jit(solution)/shard_map/all_to_all | solution.py:161
  111.2 0.0 copy-done.1
  111.2 0.0 copy-done.2
  111.2 0.0 copy-done.3
  111.3 0.7 cached_attention.1
  112.0 0.0 copy-start.4
  112.0 0.6 copy-done.4
  112.6 0.0 copy-start.5
  112.6 0.6 copy-done.5
  113.2 0.0 copy-start.6
  113.2 0.6 copy-done.6
  113.8 0.1 fusion
  113.9 0.7 pad_maximum_fusion
  114.6 1.3 %all-to-all-done.2 = bf16[4,144,128]{2,1,0:T(8,128)(2,1)S(1)} async-done(((bf16[4,144,128]{2,1,0:T(8,128)(2,1)}), bf16[4,144,128]{2,1,0:T(8,128)(2,1)S(1)}, u32[]{:S(2)}, u32[]{:S(2)}) %all-to-all-start.2) | async-done | bytes 147488 | tf_op jit(solution)/shard_map/all_to_all | solution.py:161
  115.9 0.7 broadcast_in_dim.14
  116.6 3.3 %all-to-all-start.3 = ((bf16[4,128,128]{2,1,0:T(8,128)(2,1)}), bf16[4,128,128]{2,1,0:T(8,128)(2,1)S(1)}, u32[]{:S(2)}, u32[]{:S(2)}) async-start(bf16[4,128,128]{2,1,0:T(8,128)(2,1)} %broadcast_in_dim.14), calls=%async_computation.3 | async-start | bytes 262144 | tf_op jit(solution)/shard_map/all_to_all | solution.py:135
  119.9 0.6 concatenate.13.raw_ref
  120.5 2.1 %fresh_attention.1 = (bf16[4,128]{1,0:T(4,128)(2,1)}, bf16[64,128]{1,0:T(8,128)(2,1)}) custom-call(f32[8,128]{1,0:T(8,128)} %concatenate.13.raw_ref, f32[8,128]{1,0:T(8,128)} %get-tuple-element.32.cosine_ref, f32[8,128]{1,0:T(8,128)} %get-tuple-element.33.sine_ref, bf16[64,128]{1,0:T(8,128)(2,1)} %bitcast.20, bf16[4,128]{1,0:T(4,128)(2,1)} %bitcast.24, ...), custom_call_target="tpu_custom_call" | custom-call | flops 262144 | bytes 131072 | tf_op jit(solution)/shard_map/fresh_attention/pallas_call | solution.py:124
  122.6 3.3 %all-to-all-done.3 = bf16[4,128,128]{2,1,0:T(8,128)(2,1)S(1)} async-done(((bf16[4,128,128]{2,1,0:T(8,128)(2,1)}), bf16[4,128,128]{2,1,0:T(8,128)(2,1)S(1)}, u32[]{:S(2)}, u32[]{:S(2)}) %all-to-all-start.3) | async-done | bytes 131104 | tf_op jit(solution)/shard_map/all_to_all | solution.py:135
  125.8 0.7 bitcast_convert_fusion
  (12 shorter events, 0.1 us)
Async XLA Ops:
  2.1 70.6 %all-to-all-start = ((bf16[8,128,128]{2,1,0:T(8,128)(2,1)}), bf16[8,128,128]{2,1,0:T(8,128)(2,1)S(1)}, u32[]{:S(2)}, u32[]{:S(2)}) async-start(bf16[8,128,128]{2,1,0:T(8,128)(2,1)} %broadcast_in_dim.11), calls=%async_computation | async-start | bytes 524288 | tf_op jit(solution)/shard_map/all_to_all | solution.py:135
  72.7 1.6 %copy-start = (bf16[512,2048]{1,0:T(8,128)(2,1)S(1)}, bf16[512,2048]{1,0:T(8,128)(2,1)}, u32[]{:S(2)}) copy-start(bf16[512,2048]{1,0:T(8,128)(2,1)} %probe_ref.1) | copy-start | bytes 6291460
  78.2 28.0 %all-to-all-start.1 = ((bf16[32,160,128]{2,1,0:T(8,128)(2,1)}), bf16[32,160,128]{2,1,0:T(8,128)(2,1)S(1)}, u32[]{:S(2)}, u32[]{:S(2)}) async-start(bf16[32,160,128]{2,1,0:T(8,128)(2,1)} %bitcast.2), calls=%async_computation.1 | async-start | bytes 2621440 | tf_op jit(solution)/shard_map/all_to_all | solution.py:155
  85.4 25.8 %copy-start.1 = (bf16[1,1,2048,128]{3,2,1,0:T(8,128)(2,1)S(1)}, bf16[1,1,2048,128]{3,2,1,0:T(8,128)(2,1)}, u32[]{:S(2)}) copy-start(bf16[1,1,2048,128]{3,2,1,0:T(8,128)(2,1)} %param.14) | copy-start | bytes 1572868
  85.4 25.8 %copy-start.2 = (bf16[1,1,2048,128]{3,2,1,0:T(8,128)(2,1)S(1)}, bf16[1,1,2048,128]{3,2,1,0:T(8,128)(2,1)}, u32[]{:S(2)}) copy-start(bf16[1,1,2048,128]{3,2,1,0:T(8,128)(2,1)} %param.15) | copy-start | bytes 1572868
  85.4 25.8 %copy-start.3 = (bf16[4,1,16,128]{3,2,1,0:T(8,128)(2,1)S(1)}, bf16[4,1,16,128]{3,2,1,0:T(8,128)(2,1)}, u32[]{:S(2)}) copy-start(bf16[4,1,16,128]{3,2,1,0:T(8,128)(2,1)} %param.13) | copy-start | bytes 49156
  107.2 8.7 %all-to-all-start.2 = ((bf16[4,144,128]{2,1,0:T(8,128)(2,1)}), bf16[4,144,128]{2,1,0:T(8,128)(2,1)S(1)}, u32[]{:S(2)}, u32[]{:S(2)}) async-start(bf16[4,144,128]{2,1,0:T(8,128)(2,1)} %maximum_maximum_fusion), calls=%async_computation.2 | async-start | bytes 294912 | tf_op jit(solution)/shard_map/all_to_all | solution.py:161
  112.0 0.6 copy-start.4
  112.6 0.6 copy-start.5
  113.2 0.6 copy-start.6
  116.6 9.3 %all-to-all-start.3 = ((bf16[4,128,128]{2,1,0:T(8,128)(2,1)}), bf16[4,128,128]{2,1,0:T(8,128)(2,1)S(1)}, u32[]{:S(2)}, u32[]{:S(2)}) async-start(bf16[4,128,128]{2,1,0:T(8,128)(2,1)} %broadcast_in_dim.14), calls=%async_computation.3 | async-start | bytes 262144 | tf_op jit(solution)/shard_map/all_to_all | solution.py:135

commit v3 on v1

--- a/solution.py
+++ b/solution.py
@@ -10,11 +10,13 @@
 F32 = jnp.float32
 
 FAR, NEAR, Y, X, CORES = 8, 4, 4, 4, 2
+PAIR = 2
 HEADS = X * CORES
 STEPS = 4
 HD = 128
 CHECK = 512
-SHARE = CHECK // Y
+PART = CHECK // PAIR
+SHARE = PART // Y
 SEQ_ROWS = NEAR * STEPS
 GROUP_ROWS = Y * SEQ_ROWS
 PACK = SHARE + 2 * SEQ_ROWS
@@ -25,7 +27,7 @@
     return high, (value - high.astype(F32)).astype(BF16)
 
 
-def product_kernel(block_ref, head_ref, unit_ref, hidden_ref, probe_ref, out_ref, total_ref):
+def product_kernel(block_ref, head_ref, part_ref, unit_ref, hidden_ref, probe_ref, out_ref, total_ref):
     step = pl.program_id(0)
 
     @pl.when(step == 0)
@@ -47,25 +49,25 @@
             out_ref[y, :, :SHARE] = total_ref[:, start : start + SHARE].astype(BF16)
 
 
-def products(blocks, heads, units, hidden, probes):
+def products(blocks, heads, part, units, hidden, probes):
     return pl.pallas_call(
         product_kernel,
         grid_spec=pltpu.PrefetchScalarGridSpec(
-            num_scalar_prefetch=2,
+            num_scalar_prefetch=3,
             grid=(FAR,),
             in_specs=[
-                pl.BlockSpec((1, HD, HD), lambda k, b, h: (k, 0, 0)),
-                pl.BlockSpec((GROUP_ROWS, HD), lambda k, b, h: (0, b[k])),
-                pl.BlockSpec((CHECK, HD), lambda k, b, h: (0, b[k])),
+                pl.BlockSpec((1, HD, HD), lambda k, b, h, part: (k, 0, 0)),
+                pl.BlockSpec((GROUP_ROWS, HD), lambda k, b, h, part: (0, b[k])),
+                pl.BlockSpec((PART, HD), lambda k, b, h, part: (part[0], b[k])),
             ],
-            out_specs=pl.BlockSpec((Y, HEADS, PACK, HD), lambda k, b, h: (0, 0, 0, 0)),
-            scratch_shapes=[pltpu.VMEM((HEADS, GROUP_ROWS + CHECK, HD), F32)],
+            out_specs=pl.BlockSpec((Y, HEADS, PACK, HD), lambda k, b, h, part: (0, 0, 0, 0)),
+            scratch_shapes=[pltpu.VMEM((HEADS, GROUP_ROWS + PART, HD), F32)],
         ),
         out_shape=jax.ShapeDtypeStruct((Y, HEADS, PACK, HD), BF16),
         compiler_params=pltpu.CompilerParams(vmem_limit_bytes=24 << 20),
-        cost_estimate=pl.CostEstimate(flops=2 * FAR * (GROUP_ROWS + CHECK) * HD * HD, bytes_accessed=4 << 20, transcendentals=0),
+        cost_estimate=pl.CostEstimate(flops=2 * FAR * (GROUP_ROWS + PART) * HD * HD, bytes_accessed=2 << 20, transcendentals=0),
         name="products",
-    )(blocks, heads, units, hidden, probes)
+    )(blocks, heads, part, units, hidden, probes)
 
 
 def cached_kernel(length_ref, query_ref, key_ref, value_ref, max_ref, total_ref, mixed_ref):
@@ -137,9 +139,10 @@
 def on_device(trained_units, unit_place, hidden_states, probes, queries, key_cache, value_cache, new_values, cache_lengths):
     mine = lax.axis_index("zl") * Y + lax.axis_index("y")
     places = lax.dynamic_index_in_dim(unit_place.reshape(FAR, NEAR * Y), mine, axis=1, keepdims=False)
-    units = spread(trained_units[0, 0], "zh", FAR)
-    hidden = lax.all_gather(hidden_states[:, 0], "zl", axis=0)
-    hidden = lax.all_gather(hidden, "y", axis=0).reshape(GROUP_ROWS, -1)
+    hidden = spread(hidden_states[:, 0], "zl", NEAR)
+    own_unit, hidden = lax.optimization_barrier((trained_units[0, 0], hidden))
+    units = spread(own_unit, ("zf", "zn"), FAR)
+    hidden = lax.all_gather(hidden.reshape(SEQ_ROWS, -1), "y", axis=0).reshape(GROUP_ROWS, -1)
 
     query_rows = queries.reshape(-1, HD)
     cached = cached_attention(cache_lengths, query_rows, key_cache[0, 0], value_cache[0, 0])
@@ -150,7 +153,7 @@
     cosine = jnp.concatenate([cosine, cosine], axis=1)
     sine = jnp.concatenate([-sine, sine], axis=1)
 
-    packed = products(places // HEADS, places % HEADS, units, hidden, probes)
+    packed = products(places // HEADS, places % HEADS, lax.axis_index("zn")[None], units, hidden, probes)
     packed = lax.all_to_all(packed.reshape(Y * HEADS, PACK, HD), ("y", "x", "c"), 0, 0, tiled=True)
     packed = jnp.sum(packed.astype(F32), axis=0)
     raw = packed[SHARE : SHARE + SEQ_ROWS] + packed[SHARE + SEQ_ROWS :]
@@ -161,15 +164,15 @@
     packed = jnp.sum(packed.astype(F32), axis=0)
     raw = packed[SHARE : SHARE + STEPS] + packed[SHARE + STEPS : SHARE + 2 * STEPS]
     raw = jnp.concatenate([raw, jnp.zeros_like(raw)], axis=0)
-    checksum = spread(packed[:SHARE].astype(BF16), "y", Y).reshape(CHECK, HD).astype(F32)
+    checksum = spread(packed[:SHARE].astype(BF16), ("zn", "y"), PAIR * Y).reshape(CHECK, HD).astype(F32)
 
     new_keys, attended = fresh_attention(raw, cosine, sine, query_rows, new_values.reshape(STEPS, HD), cached)
     return new_keys.reshape(STEPS, 1, 1, HD), attended.reshape(queries.shape), checksum
 
 
 def solution(mesh):
-    own = Mesh(mesh.devices.reshape(FAR, NEAR, Y, X, CORES), ("zh", "zl", "y", "x", "c"))
-    fsdp, tp = ("zh", "zl", "y"), ("x", "c")
+    own = Mesh(mesh.devices.reshape(-1, PAIR, NEAR, Y, X, CORES), ("zf", "zn", "zl", "y", "x", "c"))
+    fsdp, tp = ("zf", "zn", "zl", "y"), ("x", "c")
     return jax.shard_map(
         on_device,
         mesh=own,

time: 127 us -> 134 us (1.055)
  the two profiles are of different devices: /device:TPU:256 before, /device:TPU:2 now
where the time goes in v3:
time: 134 us; the launch traced here: 133 us
  waiting for transfers between devices  44 us (33%)
  starting transfers between devices  37.3 us (28%)
  blocking collectives  33.1 us (25%)
  local copies, waits for them, and re-layouts  7.8 us (6%)
  Pallas kernels  6.09 us (5%)
  other arithmetic  3.09 us (2%)
  between operations  1.41 us (1%)
    all_to_all x2, waiting for transfers between devices, spread(): lax.all_to_all(jnp.broadcast_to(value[None], (copies, *value.shape)), axi...  30.8 us
    all_to_all x2, starting transfers between devices, spread(): lax.all_to_all(jnp.broadcast_to(value[None], (copies, *value.shape)), axi...  29.5 us
    all_to_all x1, waiting for transfers between devices, on_device(): lax.all_to_all(packed.reshape(Y * HEADS, PACK, HD), ('y', 'x', 'c'), 0, 0...  13.2 us
    all_gather x1, blocking collectives, on_device(): lax.all_gather(hidden.reshape(SEQ_ROWS, -1), 'y', axis=0)  12.8 us
    all_to_all x1, blocking collectives, spread(): lax.all_to_all(jnp.broadcast_to(value[None], (copies, *value.shape)), axi...  11.4 us
    all_to_all x1, blocking collectives, on_device(): packed = lax.all_to_all(packed, 'zl', 0, 0, tiled=True)  8.88 us
    all_to_all x1, starting transfers between devices, on_device(): lax.all_to_all(packed.reshape(Y * HEADS, PACK, HD), ('y', 'x', 'c'), 0, 0...  7.75 us
    unnamed x15, local copies, waits for them, and re-layouts  3.91 us
  transfers between devices with their start and end apart: 3, of which 3 were waited for; matrix products, arithmetic and copies ran while one was open for 3% of the time, Pallas kernels for 2%

profile of v3, /device:TPU:2, one launch (start us, length us, event | category | flops | bytes accessed | tf_op | source)
XLA Modules:
  0.0 132.8 jit_solution(15403906588902198379)
XLA Ops:
  0.6 0.7 broadcast_in_dim.16
  1.4 11.4 %all_to_all.25 = bf16[4,4,2048]{2,1,0:T(4,128)(2,1)S(1)} all-to-all(bf16[4,4,2048]{2,1,0:T(4,128)(2,1)S(1)} %broadcast_in_dim.16), channel_id=1, replica_groups=mesh['zf'=4,'zn'=2,'zl'=4,'y'=4,'x'=4,'c'=2] {'zl'}, dimensions={0} | all-to-all | bytes 131072 | tf_op jit(solution)/shard_map/all_to_all | solution.py:136
  12.8 1.5 %broadcast_in_dim.17 = bf16[8,128,128]{2,1,0:T(8,128)(2,1)} broadcast(bf16[128,128]{1,0:T(8,128)(2,1)} %bitcast.24), dimensions={1,2} | broadcast | bytes 294912 | tf_op jit(solution)/shard_map/broadcast_in_dim | solution.py:136
  14.3 25.6 %all-to-all-start.1 = ((bf16[8,128,128]{2,1,0:T(8,128)(2,1)}), bf16[8,128,128]{2,1,0:T(8,128)(2,1)S(1)}, u32[]{:S(2)}, u32[]{:S(2)}) async-start(bf16[8,128,128]{2,1,0:T(8,128)(2,1)} %broadcast_in_dim.17), calls=%async_computation.1 | async-start | bytes 524288 | tf_op jit(solution)/shard_map/all_to_all | solution.py:136
  40.0 0.5 broadcast.54
  40.5 1.3 reduce.5
  41.8 0.1 reshape.49
  41.9 0.2 dynamic-slice_reduce_fusion
  42.1 12.8 %all_gather.3 = bf16[4,16,2048]{2,1,0:T(8,128)(2,1)S(1)} all-gather(bf16[1,16,2048]{2,1,0:T(8,128)(2,1)S(1)} %all_gather_reshape.3), channel_id=1, replica_groups=mesh['zf'=4,'zn'=2,'zl'=4,'y'=4,'x'=4,'c'=2] {'y'}, dimensions={0}, use_global_device_ids=true | all-gather | bytes 327680 | tf_op jit(solution)/shard_map/all_gather | solution.py:145
  54.9 23.5 %all-to-all-done.1.unit_ref = bf16[8,128,128]{2,1,0:T(8,128)(2,1)S(1)} async-done(((bf16[8,128,128]{2,1,0:T(8,128)(2,1)}), bf16[8,128,128]{2,1,0:T(8,128)(2,1)S(1)}, u32[]{:S(2)}, u32[]{:S(2)}) %all-to-all-start.1) | async-done | bytes 262176 | tf_op jit(solution)/shard_map/all_to_all | solution.py:136
  78.4 0.0 copy-start
  78.4 1.6 %copy-done = bf16[512,2048]{1,0:T(8,128)(2,1)S(1)} copy-done((bf16[512,2048]{1,0:T(8,128)(2,1)S(1)}, bf16[512,2048]{1,0:T(8,128)(2,1)}, u32[]{:S(2)}) %copy-start) | copy-done | bytes 2097176
  80.0 3.3 %products.1 = bf16[4,8,96,128]{3,2,1,0:T(8,128)(2,1)} custom-call(s32[8]{0:T(128)S(1)} %get-tuple-element.35.block_ref, s32[8]{0:T(128)S(1)} %get-tuple-element.34.head_ref, s32[1]{0:T(128)} %bitcast.part_ref, bf16[8,128,128]{2,1,0:T(8,128)(2,1)S(1)} %all-to-all-done.1.unit_ref, bf16[64,2048]{1,0:T(8,128)(2,1)S(1)} %bitcast.19, bf16[512,2048]{1,0:T(8,128)(2,1)S(1)} %copy-done), custom_call_target="tpu_custom_call" | custom-call | flops 83886080 | bytes 2097152 | tf_op jit(solution)/shard_map/products/pallas_call | solution.py:53
  83.3 0.0 copy-start.1
  83.3 0.0 copy-start.2
  83.3 0.0 copy-start.3
  83.3 7.7 %all-to-all-start.2 = ((bf16[32,96,128]{2,1,0:T(8,128)(2,1)}), bf16[32,96,128]{2,1,0:T(8,128)(2,1)S(1)}, u32[]{:S(2)}, u32[]{:S(2)}) async-start(bf16[32,96,128]{2,1,0:T(8,128)(2,1)} %bitcast.4), calls=%async_computation.2 | async-start | bytes 1572864 | tf_op jit(solution)/shard_map/all_to_all | solution.py:157
  91.1 0.1 pad.8.clone
  91.2 13.2 %all-to-all-done.2 = bf16[32,96,128]{2,1,0:T(8,128)(2,1)S(1)} async-done(((bf16[32,96,128]{2,1,0:T(8,128)(2,1)}), bf16[32,96,128]{2,1,0:T(8,128)(2,1)S(1)}, u32[]{:S(2)}, u32[]{:S(2)}) %all-to-all-start.2) | async-done | bytes 786464 | tf_op jit(solution)/shard_map/all_to_all | solution.py:157
  104.4 0.1 convert_reduce_fusion
  104.6 0.1 maximum_maximum_fusion
  104.7 8.9 %all_to_all.26 = bf16[4,80,128]{2,1,0:T(8,128)(2,1)S(1)} all-to-all(bf16[4,80,128]{2,1,0:T(8,128)(2,1)S(1)} %maximum_maximum_fusion), channel_id=1, replica_groups=mesh['zf'=4,'zn'=2,'zl'=4,'y'=4,'x'=4,'c'=2] {'zl'}, dimensions={0} | all-to-all | bytes 163840 | tf_op jit(solution)/shard_map/all_to_all | solution.py:163
  113.6 0.7 broadcast_in_dim.40
  114.2 3.9 %all-to-all-start.4 = ((bf16[8,64,128]{2,1,0:T(8,128)(2,1)}), bf16[8,64,128]{2,1,0:T(8,128)(2,1)S(1)}, u32[]{:S(2)}, u32[]{:S(2)}) async-start(bf16[8,64,128]{2,1,0:T(8,128)(2,1)} %broadcast_in_dim.40), calls=%async_computation.4 | async-start | bytes 262144 | tf_op jit(solution)/shard_map/all_to_all | solution.py:136
  118.8 0.0 copy-done.1
  118.8 0.0 copy-done.2
  118.8 0.0 copy-done.3
  118.8 0.7 cached_attention.1
  119.5 0.0 copy-start.4
  119.6 0.6 copy-done.4
  120.1 0.0 copy-start.5
  120.1 0.6 copy-done.5
  120.7 0.0 copy-start.6
  120.8 0.6 copy-done.6
  121.4 0.1 fusion
  121.5 0.7 pad_maximum_fusion
  122.2 0.6 concatenate.13.raw_ref
  122.8 2.1 %fresh_attention.1 = (bf16[4,128]{1,0:T(4,128)(2,1)}, bf16[64,128]{1,0:T(8,128)(2,1)}) custom-call(f32[8,128]{1,0:T(8,128)} %concatenate.13.raw_ref, f32[8,128]{1,0:T(8,128)} %get-tuple-element.36.cosine_ref, f32[8,128]{1,0:T(8,128)} %get-tuple-element.37.sine_ref, bf16[64,128]{1,0:T(8,128)(2,1)} %bitcast.22, bf16[4,128]{1,0:T(4,128)(2,1)} %bitcast.27, ...), custom_call_target="tpu_custom_call" | custom-call | flops 262144 | bytes 131072 | tf_op jit(solution)/shard_map/fresh_attention/pallas_call | solution.py:125
  124.8 7.2 %all-to-all-done.4 = bf16[8,64,128]{2,1,0:T(8,128)(2,1)S(1)} async-done(((bf16[8,64,128]{2,1,0:T(8,128)(2,1)}), bf16[8,64,128]{2,1,0:T(8,128)(2,1)S(1)}, u32[]{:S(2)}, u32[]{:S(2)}) %all-to-all-start.4) | async-done | bytes 131104 | tf_op jit(solution)/shard_map/all_to_all | solution.py:136
  132.1 0.7 bitcast_convert_fusion
  (12 shorter events, 0.1 us)
Async XLA Ops:
  14.3 64.1 %all-to-all-start.1 = ((bf16[8,128,128]{2,1,0:T(8,128)(2,1)}), bf16[8,128,128]{2,1,0:T(8,128)(2,1)S(1)}, u32[]{:S(2)}, u32[]{:S(2)}) async-start(bf16[8,128,128]{2,1,0:T(8,128)(2,1)} %broadcast_in_dim.17), calls=%async_computation.1 | async-start | bytes 524288 | tf_op jit(solution)/shard_map/all_to_all | solution.py:136
  78.4 1.6 %copy-start = (bf16[512,2048]{1,0:T(8,128)(2,1)S(1)}, bf16[512,2048]{1,0:T(8,128)(2,1)}, u32[]{:S(2)}) copy-start(bf16[512,2048]{1,0:T(8,128)(2,1)} %probe_ref.1) | copy-start | bytes 6291460
  83.3 35.5 %copy-start.1 = (bf16[1,1,2048,128]{3,2,1,0:T(8,128)(2,1)S(1)}, bf16[1,1,2048,128]{3,2,1,0:T(8,128)(2,1)}, u32[]{:S(2)}) copy-start(bf16[1,1,2048,128]{3,2,1,0:T(8,128)(2,1)} %param.14) | copy-start | bytes 1572868
  83.3 35.5 %copy-start.2 = (bf16[1,1,2048,128]{3,2,1,0:T(8,128)(2,1)S(1)}, bf16[1,1,2048,128]{3,2,1,0:T(8,128)(2,1)}, u32[]{:S(2)}) copy-start(bf16[1,1,2048,128]{3,2,1,0:T(8,128)(2,1)} %param.15) | copy-start | bytes 1572868
  83.3 35.5 %copy-start.3 = (bf16[4,1,16,128]{3,2,1,0:T(8,128)(2,1)S(1)}, bf16[4,1,16,128]{3,2,1,0:T(8,128)(2,1)}, u32[]{:S(2)}) copy-start(bf16[4,1,16,128]{3,2,1,0:T(8,128)(2,1)} %param.13) | copy-start | bytes 49156
  83.3 21.1 %all-to-all-start.2 = ((bf16[32,96,128]{2,1,0:T(8,128)(2,1)}), bf16[32,96,128]{2,1,0:T(8,128)(2,1)S(1)}, u32[]{:S(2)}, u32[]{:S(2)}) async-start(bf16[32,96,128]{2,1,0:T(8,128)(2,1)} %bitcast.4), calls=%async_computation.2 | async-start | bytes 1572864 | tf_op jit(solution)/shard_map/all_to_all | solution.py:157
  114.2 17.8 %all-to-all-start.4 = ((bf16[8,64,128]{2,1,0:T(8,128)(2,1)}), bf16[8,64,128]{2,1,0:T(8,128)(2,1)S(1)}, u32[]{:S(2)}, u32[]{:S(2)}) async-start(bf16[8,64,128]{2,1,0:T(8,128)(2,1)} %broadcast_in_dim.40), calls=%async_computation.4 | async-start | bytes 262144 | tf_op jit(solution)/shard_map/all_to_all | solution.py:136
  119.5 0.6 copy-start.4
  120.1 0.6 copy-start.5
  120.7 0.6 copy-start.6

commit v4 on v2

--- a/solution.py
+++ b/solution.py
@@ -25,30 +25,37 @@
     return high, (value - high.astype(F32)).astype(BF16)
 
 
-def product_kernel(block_ref, head_ref, unit_ref, hidden_ref, probe_ref, out_ref, total_ref):
+def product_kernel(place_ref, spot_ref, unit_ref, hidden_ref, probe_ref, kept_ref, sent_ref, total_ref):
     step = pl.program_id(0)
 
     @pl.when(step == 0)
     def _():
         total_ref[...] = jnp.zeros_like(total_ref)
 
-    head = head_ref[step]
+    head = lax.rem(place_ref[step * NEAR * Y + spot_ref[0]], HEADS)
+    slot = lax.rem(head + spot_ref[1], CORES) * X + lax.div(head, CORES)
     unit = unit_ref[0]
-    total_ref[head, :GROUP_ROWS] += jnp.dot(hidden_ref[...], unit, preferred_element_type=F32)
-    total_ref[head, GROUP_ROWS:] += jnp.dot(probe_ref[...], unit, preferred_element_type=F32)
+    total_ref[slot, :GROUP_ROWS] += jnp.dot(hidden_ref[...], unit, preferred_element_type=F32)
+    total_ref[slot, GROUP_ROWS:] += jnp.dot(probe_ref[...], unit, preferred_element_type=F32)
 
     @pl.when(step == FAR - 1)
     def _():
         for y in range(Y):
             starts = [(plane * Y + y) * STEPS for plane in range(NEAR)]
-            high, low = split_sum(jnp.concatenate([total_ref[:, start : start + STEPS] for start in starts], axis=1))
-            out_ref[y, :, SHARE : SHARE + SEQ_ROWS] = high
-            out_ref[y, :, SHARE + SEQ_ROWS :] = low
+            tokens = jnp.concatenate([total_ref[:, start : start + STEPS] for start in starts], axis=1)
             start = GROUP_ROWS + y * SHARE
-            out_ref[y, :, :SHARE] = total_ref[:, start : start + SHARE].astype(BF16)
-
-
-def products(blocks, heads, units, hidden, probes):
+            kept_ref[y, :, :SHARE] = total_ref[:X, start : start + SHARE]
+            kept_ref[y, :, SHARE:] = tokens[:X]
+            high, low = split_sum(tokens[X:])
+            sent_ref[y, :, :SHARE] = total_ref[X:, start : start + SHARE].astype(BF16)
+            sent_ref[y, :, SHARE : SHARE + SEQ_ROWS] = high
+            sent_ref[y, :, SHARE + SEQ_ROWS :] = low
+
+
+def products(places, spot, units, hidden, probes):
+    def block(k, place, spot):
+        return 0, lax.div(place[k * NEAR * Y + spot[0]], HEADS)
+
     return pl.pallas_call(
         product_kernel,
         grid_spec=pltpu.PrefetchScalarGridSpec(
@@ -56,17 +63,48 @@
             grid=(FAR,),
             in_specs=[
                 pl.BlockSpec((1, HD, HD), lambda k, b, h: (k, 0, 0)),
-                pl.BlockSpec((GROUP_ROWS, HD), lambda k, b, h: (0, b[k])),
-                pl.BlockSpec((CHECK, HD), lambda k, b, h: (0, b[k])),
+                pl.BlockSpec((GROUP_ROWS, HD), block),
+                pl.BlockSpec((CHECK, HD), block),
             ],
-            out_specs=pl.BlockSpec((Y, HEADS, PACK, HD), lambda k, b, h: (0, 0, 0, 0)),
+            out_specs=[
+                pl.BlockSpec((Y, X, SHARE + SEQ_ROWS, HD), lambda k, b, h: (0, 0, 0, 0)),
+                pl.BlockSpec((Y, X, PACK, HD), lambda k, b, h: (0, 0, 0, 0)),
+            ],
             scratch_shapes=[pltpu.VMEM((HEADS, GROUP_ROWS + CHECK, HD), F32)],
         ),
-        out_shape=jax.ShapeDtypeStruct((Y, HEADS, PACK, HD), BF16),
+        out_shape=[
+            jax.ShapeDtypeStruct((Y, X, SHARE + SEQ_ROWS, HD), F32),
+            jax.ShapeDtypeStruct((Y, X, PACK, HD), BF16),
+        ],
         compiler_params=pltpu.CompilerParams(vmem_limit_bytes=24 << 20),
         cost_estimate=pl.CostEstimate(flops=2 * FAR * (GROUP_ROWS + CHECK) * HD * HD, bytes_accessed=4 << 20, transcendentals=0),
         name="products",
-    )(blocks, heads, units, hidden, probes)
+    )(places, spot, units, hidden, probes)
+
+
+def join_kernel(kept_ref, sent_ref, out_ref):
+    sent = sent_ref[...].astype(F32)
+    out_ref[:, :, :SHARE] = (kept_ref[:, :, :SHARE] + sent[:, :, :SHARE]).astype(BF16)
+    tokens = kept_ref[:, :, SHARE:] + sent[:, :, SHARE : SHARE + SEQ_ROWS] + sent[:, :, SHARE + SEQ_ROWS :]
+    high, low = split_sum(tokens)
+    out_ref[:, :, SHARE : SHARE + SEQ_ROWS] = high
+    out_ref[:, :, SHARE + SEQ_ROWS :] = low
+
+
+def join_cores(kept, sent):
+    return pl.pallas_call(
+        join_kernel,
+        grid=(Y,),
+        in_specs=[
+            pl.BlockSpec((1, X, SHARE + SEQ_ROWS, HD), lambda y: (y, 0, 0, 0)),
+            pl.BlockSpec((1, X, PACK, HD), lambda y: (y, 0, 0, 0)),
+        ],
+        out_specs=pl.BlockSpec((1, X, PACK, HD), lambda y: (y, 0, 0, 0)),
+        out_shape=jax.ShapeDtypeStruct((Y, X, PACK, HD), BF16),
+        compiler_params=pltpu.CompilerParams(vmem_limit_bytes=24 << 20),
+        cost_estimate=pl.CostEstimate(flops=1 << 20, bytes_accessed=3 << 20, transcendentals=0),
+        name="join_cores",
+    )(kept, sent)
 
 
 def cached_kernel(length_ref, query_ref, key_ref, value_ref, max_ref, total_ref, mixed_ref):
@@ -136,11 +174,9 @@
 
 
 def on_device(trained_units, unit_place, hidden_states, probes, queries, key_cache, value_cache, new_values, cache_lengths):
-    mine = lax.axis_index("zl") * Y + lax.axis_index("y")
-    places = lax.dynamic_index_in_dim(unit_place.reshape(FAR, NEAR * Y), mine, axis=1, keepdims=False)
-    units = spread(trained_units[0, 0], "zh", FAR)
-    hidden = lax.all_gather(hidden_states[:, 0], "y", axis=0).reshape(Y * STEPS, -1)
-    hidden = lax.all_gather(hidden, "zl", axis=0).reshape(GROUP_ROWS, -1)
+    spot = lax.axis_index("zl") * Y + lax.axis_index("y")
+    hidden = spread(hidden_states[:, 0], ("zl", "y"), NEAR * Y).reshape(GROUP_ROWS, -1)
+    units = lax.all_gather(trained_units[0, 0], "zh", axis=0)
 
     query_rows = queries.reshape(-1, HD)
     cached = cached_attention(cache_lengths, query_rows, key_cache[0, 0], value_cache[0, 0])
@@ -151,8 +187,11 @@
     cosine = jnp.concatenate([cosine, cosine], axis=1)
     sine = jnp.concatenate([-sine, sine], axis=1)
 
-    packed = products(places // HEADS, places % HEADS, units, hidden, probes)
-    packed = lax.all_to_all(packed.reshape(Y * HEADS, PACK, HD), ("y", "x", "c"), 0, 0, tiled=True)
+    spot = jnp.stack([spot, lax.axis_index("c")])
+    kept, sent = products(unit_place[0], spot, units, hidden, probes)
+    sent = lax.ppermute(sent, "c", [(core, CORES - 1 - core) for core in range(CORES)])
+    packed = join_cores(kept, sent)
+    packed = lax.all_to_all(packed.reshape(Y * X, PACK, HD), ("y", "x"), 0, 0, tiled=True)
     packed = jnp.sum(packed.astype(F32), axis=0)
     raw = packed[SHARE : SHARE + SEQ_ROWS] + packed[SHARE + SEQ_ROWS :]
     share = jnp.broadcast_to(packed[None, :SHARE].astype(BF16), (NEAR, SHARE, HD))

time: 127 us -> 116 us (0.913)
  waiting for transfers between devices: 34.5 us -> 19.8 us
  blocking collectives: 30.9 us -> 43.9 us
  starting transfers between devices: 41.3 us -> 33.6 us
  local copies, waits for them, and re-layouts: 7.86 us -> 6.38 us
  other arithmetic: 3.84 us -> 2.5 us
    all_gather x2 -> x1, blocking collectives: 30.9 us -> 43.9 us  [on_device(): units = lax.all_gather(trained_units[0, 0], 'zh', axis=0)]
    all_to_all x2, starting transfers between devices: 30.8 us -> 19.4 us  [spread(): lax.all_to_all(jnp.broadcast_to(value[None], (copies, *value.shape)), axi...]
    all_to_all x2, waiting for transfers between devices: 12.6 us -> 3.28 us  [spread(): lax.all_to_all(jnp.broadcast_to(value[None], (copies, *value.shape)), axi...]
    all_to_all x1, waiting for transfers between devices: 20.7 us -> 13.2 us  [on_device(): lax.all_to_all(packed.reshape(Y * X, PACK, HD), ('y', 'x'), 0, 0, tiled=T...]
    ppermute x0 -> x1, waiting for transfers between devices: none -> 2.06 us  [on_device(): lax.ppermute(sent, 'c', [(core, CORES - 1 - core) for core in range(CORES)])]
    ppermute x0 -> x1, starting transfers between devices: none -> 1.92 us  [on_device(): lax.ppermute(sent, 'c', [(core, CORES - 1 - core) for core in range(CORES)])]
    all_to_all x1, starting transfers between devices: 3.39 us -> 4.98 us  [on_device(): packed = lax.all_to_all(packed, 'zl', 0, 0, tiled=True)]
    pallas_call x0 -> x1, Pallas kernels: none -> 1.49 us  [join_cores(): pl.pallas_call(join_kernel, grid=(Y,), in_specs=[pl.BlockSpec((1, X, SHAR...]
  transfers between devices with their start and end apart: 4 -> 5, of which waited for: 4 -> 4; matrix products, arithmetic and copies ran while one was open for 3% -> 1% of each run, Pallas kernels for 2% -> 2%
where the time goes in v4:
time: 116 us; the launch traced here: 115 us
  blocking collectives  43.9 us (38%)
  starting transfers between devices  33.6 us (29%)
  waiting for transfers between devices  19.8 us (17%)
  Pallas kernels  7.27 us (6%)
  local copies, waits for them, and re-layouts  6.38 us (6%)
  other arithmetic  2.5 us (2%)
  between operations  1.46 us (1%)
    all_gather x1, blocking collectives, on_device(): units = lax.all_gather(trained_units[0, 0], 'zh', axis=0)  43.9 us
    all_to_all x2, starting transfers between devices, spread(): lax.all_to_all(jnp.broadcast_to(value[None], (copies, *value.shape)), axi...  19.4 us
    all_to_all x1, waiting for transfers between devices, on_device(): lax.all_to_all(packed.reshape(Y * X, PACK, HD), ('y', 'x'), 0, 0, tiled=T...  13.2 us
    all_to_all x1, starting transfers between devices, on_device(): lax.all_to_all(packed.reshape(Y * X, PACK, HD), ('y', 'x'), 0, 0, tiled=T...  7.23 us
    all_to_all x1, starting transfers between devices, on_device(): packed = lax.all_to_all(packed, 'zl', 0, 0, tiled=True)  4.98 us
    unnamed x16, local copies, waits for them, and re-layouts  3.41 us
    all_to_all x2, waiting for transfers between devices, spread(): lax.all_to_all(jnp.broadcast_to(value[None], (copies, *value.shape)), axi...  3.28 us
    pallas_call x1, Pallas kernels, products(): pl.pallas_call(product_kernel, grid_spec=pltpu.PrefetchScalarGridSpec(num...  3.01 us
  transfers between devices with their start and end apart: 5, of which 4 were waited for; matrix products, arithmetic and copies ran while one was open for 1% of the time, Pallas kernels for 2%

profile of v4, /device:TPU:32, one launch (start us, length us, event | category | flops | bytes accessed | tf_op | source)
XLA Modules:
  0.0 114.8 jit_solution(14084853441239906569)
XLA Ops:
  0.6 0.0 copy-start.7
  0.6 1.5 %broadcast_in_dim.11 = bf16[16,4,2048]{2,1,0:T(4,128)(2,1)} broadcast(bf16[4,2048]{1,0:T(4,128)(2,1)} %bitcast.27), dimensions={1,2} | broadcast | bytes 278528 | tf_op jit(solution)/shard_map/broadcast_in_dim | solution.py:173
  2.2 16.1 %all-to-all-start = ((bf16[16,4,2048]{2,1,0:T(4,128)(2,1)}), bf16[16,4,2048]{2,1,0:T(4,128)(2,1)S(1)}, u32[]{:S(2)}, u32[]{:S(2)}) async-start(bf16[16,4,2048]{2,1,0:T(4,128)(2,1)} %broadcast_in_dim.11), calls=%async_computation | async-start | bytes 524288 | tf_op jit(solution)/shard_map/all_to_all | solution.py:173
  18.3 0.1 pad_add_fusion.spot_ref
  18.3 43.9 %all-gather = bf16[8,1,128,128]{3,2,1,0:T(8,128)(2,1)S(1)} all-gather(bf16[1,1,128,128]{3,2,1,0:T(8,128)(2,1)} %param.9), channel_id=2, replica_groups=mesh['zh'=8,'zl'=4,'y'=4,'x'=4,'c'=2] {'zh'}, dimensions={0}, use_global_device_ids=true | all-gather | bytes 294912 | tf_op jit(solution)/shard_map/all_gather | solution.py:179
  62.2 0.0 all-to-all-done
  62.2 0.1 reshape.45.hidden_ref
  62.3 0.0 copy-done.7
  62.3 0.0 copy-start
  62.3 1.6 %copy-done = bf16[512,2048]{1,0:T(8,128)(2,1)S(1)} copy-done((bf16[512,2048]{1,0:T(8,128)(2,1)S(1)}, bf16[512,2048]{1,0:T(8,128)(2,1)}, u32[]{:S(2)}) %copy-start) | copy-done | bytes 2097176
  63.9 3.0 %products.1 = (f32[4,4,144,128]{3,2,1,0:T(8,128)S(1)}, bf16[4,4,160,128]{3,2,1,0:T(8,128)(2,1)S(1)}) custom-call(s32[128]{0:T(128)S(1)} %bitcast.25, s32[2]{0:T(128)S(1)} %pad_add_fusion.spot_ref, bf16[8,128,128]{2,1,0:T(8,128)(2,1)S(1)} %bitcast.20, bf16[64,2048]{1,0:T(8,128)(2,1)S(1)} %reshape.45.hidden_ref, bf16[512,2048]{1,0:T(8,128)(2,1)S(1)} %copy-done), custom_call_target="tpu_custom_call" | custom-call | flops 150994944 | bytes 4194304 | tf_op jit(solution)/shard_map/products/pallas_call | solution.py:59
  66.9 1.9 %collective-permute-start = (bf16[4,4,160,128]{3,2,1,0:T(8,128)(2,1)S(1)}, bf16[4,4,160,128]{3,2,1,0:T(8,128)(2,1)S(1)}, u32[]{:S(2)}, u32[]{:S(2)}) collective-permute-start(bf16[4,4,160,128]{3,2,1,0:T(8,128)(2,1)S(1)} %get-tuple-element.11), channel_id=1, source_target_pairs={{0,1},{1,0},{2,3},{3,2},{4,5},{5,4},{6,7},{7,6},{8,9},{9,8},{10,11... | collective-permute-start | bytes 1966088 | tf_op jit(solution)/shard_map/ppermute | solution.py:192
  68.8 2.1 %collective-permute-done.sent_ref = bf16[4,4,160,128]{3,2,1,0:T(8,128)(2,1)S(1)} collective-permute-done((bf16[4,4,160,128]{3,2,1,0:T(8,128)(2,1)S(1)}, bf16[4,4,160,128]{3,2,1,0:T(8,128)(2,1)S(1)}, u32[]{:S(2)}, u32[]{:S(2)}) %collective-permute-start) | collective-permute-done | bytes 655392 | tf_op jit(solution)/shard_map/ppermute | solution.py:192
  70.9 1.5 %join_cores.1 = bf16[4,4,160,128]{3,2,1,0:T(8,128)(2,1)} custom-call(f32[4,4,144,128]{3,2,1,0:T(8,128)S(1)} %get-tuple-element.10.kept_ref, bf16[4,4,160,128]{3,2,1,0:T(8,128)(2,1)S(1)} %collective-permute-done.sent_ref), custom_call_target="tpu_custom_call" | custom-call | flops 1048576 | bytes 3145728 | tf_op jit(solution)/shard_map/join_cores/pallas_call | solution.py:95
  72.4 0.0 copy-start.1
  72.4 0.0 copy-start.2
  72.4 0.0 copy-start.3
  72.4 7.2 %all-to-all-start.1 = ((bf16[16,160,128]{2,1,0:T(8,128)(2,1)}), bf16[16,160,128]{2,1,0:T(8,128)(2,1)S(1)}, u32[]{:S(2)}, u32[]{:S(2)}) async-start(bf16[16,160,128]{2,1,0:T(8,128)(2,1)} %bitcast.5), calls=%async_computation.1 | async-start | bytes 1310720 | tf_op jit(solution)/shard_map/all_to_all | solution.py:194
  79.7 0.1 pad.8.clone
  79.7 13.2 %all-to-all-done.1 = bf16[16,160,128]{2,1,0:T(8,128)(2,1)S(1)} async-done(((bf16[16,160,128]{2,1,0:T(8,128)(2,1)}), bf16[16,160,128]{2,1,0:T(8,128)(2,1)S(1)}, u32[]{:S(2)}, u32[]{:S(2)}) %all-to-all-start.1) | async-done | bytes 655392 | tf_op jit(solution)/shard_map/all_to_all | solution.py:194
  92.9 0.1 convert_reduce_fusion
  93.0 0.8 maximum_maximum_fusion
  93.8 5.0 %all-to-all-start.2 = ((bf16[4,144,128]{2,1,0:T(8,128)(2,1)}), bf16[4,144,128]{2,1,0:T(8,128)(2,1)S(1)}, u32[]{:S(2)}, u32[]{:S(2)}) async-start(bf16[4,144,128]{2,1,0:T(8,128)(2,1)} %maximum_maximum_fusion), calls=%async_computation.2 | async-start | bytes 294912 | tf_op jit(solution)/shard_map/all_to_all | solution.py:200
  99.4 0.0 copy-done.1
  99.4 0.0 copy-done.2
  99.5 0.0 copy-done.3
  99.5 0.7 cached_attention.1
  100.2 0.0 copy-start.4
  100.2 0.6 copy-done.4
  100.8 0.0 copy-start.5
  100.8 0.6 copy-done.5
  101.4 0.0 copy-start.6
  101.4 0.6 copy-done.6
  102.0 0.1 fusion
  102.1 0.7 pad_maximum_fusion
  102.8 1.3 %all-to-all-done.2 = bf16[4,144,128]{2,1,0:T(8,128)(2,1)S(1)} async-done(((bf16[4,144,128]{2,1,0:T(8,128)(2,1)}), bf16[4,144,128]{2,1,0:T(8,128)(2,1)S(1)}, u32[]{:S(2)}, u32[]{:S(2)}) %all-to-all-start.2) | async-done | bytes 147488 | tf_op jit(solution)/shard_map/all_to_all | solution.py:200
  104.1 0.7 broadcast_in_dim.14
  104.8 3.3 %all-to-all-start.3 = ((bf16[4,128,128]{2,1,0:T(8,128)(2,1)}), bf16[4,128,128]{2,1,0:T(8,128)(2,1)S(1)}, u32[]{:S(2)}, u32[]{:S(2)}) async-start(bf16[4,128,128]{2,1,0:T(8,128)(2,1)} %broadcast_in_dim.14), calls=%async_computation.3 | async-start | bytes 262144 | tf_op jit(solution)/shard_map/all_to_all | solution.py:173
  108.1 0.6 concatenate.13.raw_ref
  108.7 2.1 %fresh_attention.1 = (bf16[4,128]{1,0:T(4,128)(2,1)}, bf16[64,128]{1,0:T(8,128)(2,1)}) custom-call(f32[8,128]{1,0:T(8,128)} %concatenate.13.raw_ref, f32[8,128]{1,0:T(8,128)} %get-tuple-element.31.cosine_ref, f32[8,128]{1,0:T(8,128)} %get-tuple-element.32.sine_ref, bf16[64,128]{1,0:T(8,128)(2,1)} %bitcast.23, bf16[4,128]{1,0:T(4,128)(2,1)} %bitcast.28, ...), custom_call_target="tpu_custom_call" | custom-call | flops 262144 | bytes 131072 | tf_op jit(solution)/shard_map/fresh_attention/pallas_call | solution.py:162
  110.8 3.3 %all-to-all-done.3 = bf16[4,128,128]{2,1,0:T(8,128)(2,1)S(1)} async-done(((bf16[4,128,128]{2,1,0:T(8,128)(2,1)}), bf16[4,128,128]{2,1,0:T(8,128)(2,1)S(1)}, u32[]{:S(2)}, u32[]{:S(2)}) %all-to-all-start.3) | async-done | bytes 131104 | tf_op jit(solution)/shard_map/all_to_all | solution.py:173
  114.1 0.7 bitcast_convert_fusion
  (10 shorter events, 0.1 us)
Async XLA Ops:
  0.6 61.7 %copy-start.7 = (s32[1,128]{1,0:T(1,128)S(1)}, s32[1,128]{1,0:T(1,128)}, u32[]{:S(2)}) copy-start(s32[1,128]{1,0:T(1,128)} %param.10) | copy-start | bytes 1540
  2.2 60.1 %all-to-all-start = ((bf16[16,4,2048]{2,1,0:T(4,128)(2,1)}), bf16[16,4,2048]{2,1,0:T(4,128)(2,1)S(1)}, u32[]{:S(2)}, u32[]{:S(2)}) async-start(bf16[16,4,2048]{2,1,0:T(4,128)(2,1)} %broadcast_in_dim.11), calls=%async_computation | async-start | bytes 524288 | tf_op jit(solution)/shard_map/all_to_all | solution.py:173
  62.3 1.6 %copy-start = (bf16[512,2048]{1,0:T(8,128)(2,1)S(1)}, bf16[512,2048]{1,0:T(8,128)(2,1)}, u32[]{:S(2)}) copy-start(bf16[512,2048]{1,0:T(8,128)(2,1)} %probe_ref.1) | copy-start | bytes 6291460
  66.9 4.0 %collective-permute-start = (bf16[4,4,160,128]{3,2,1,0:T(8,128)(2,1)S(1)}, bf16[4,4,160,128]{3,2,1,0:T(8,128)(2,1)S(1)}, u32[]{:S(2)}, u32[]{:S(2)}) collective-permute-start(bf16[4,4,160,128]{3,2,1,0:T(8,128)(2,1)S(1)} %get-tuple-element.11), channel_id=1, source_target_pairs={{0,1},{1,0},{2,3},{3,2},{4,5},{5,4},{6,7},{7,6},{8,9},{9,8},{10,11... | collective-permute-start | bytes 1966088 | tf_op jit(solution)/shard_map/ppermute | solution.py:192
  72.4 27.0 %copy-start.1 = (bf16[1,1,2048,128]{3,2,1,0:T(8,128)(2,1)S(1)}, bf16[1,1,2048,128]{3,2,1,0:T(8,128)(2,1)}, u32[]{:S(2)}) copy-start(bf16[1,1,2048,128]{3,2,1,0:T(8,128)(2,1)} %param.14) | copy-start | bytes 1572868
  72.4 27.0 %copy-start.2 = (bf16[1,1,2048,128]{3,2,1,0:T(8,128)(2,1)S(1)}, bf16[1,1,2048,128]{3,2,1,0:T(8,128)(2,1)}, u32[]{:S(2)}) copy-start(bf16[1,1,2048,128]{3,2,1,0:T(8,128)(2,1)} %param.15) | copy-start | bytes 1572868
  72.4 27.0 %copy-start.3 = (bf16[4,1,16,128]{3,2,1,0:T(8,128)(2,1)S(1)}, bf16[4,1,16,128]{3,2,1,0:T(8,128)(2,1)}, u32[]{:S(2)}) copy-start(bf16[4,1,16,128]{3,2,1,0:T(8,128)(2,1)} %param.13) | copy-start | bytes 49156
  72.4 20.5 %all-to-all-start.1 = ((bf16[16,160,128]{2,1,0:T(8,128)(2,1)}), bf16[16,160,128]{2,1,0:T(8,128)(2,1)S(1)}, u32[]{:S(2)}, u32[]{:S(2)}) async-start(bf16[16,160,128]{2,1,0:T(8,128)(2,1)} %bitcast.5), calls=%async_computation.1 | async-start | bytes 1310720 | tf_op jit(solution)/shard_map/all_to_all | solution.py:194
  93.8 10.3 %all-to-all-start.2 = ((bf16[4,144,128]{2,1,0:T(8,128)(2,1)}), bf16[4,144,128]{2,1,0:T(8,128)(2,1)S(1)}, u32[]{:S(2)}, u32[]{:S(2)}) async-start(bf16[4,144,128]{2,1,0:T(8,128)(2,1)} %maximum_maximum_fusion), calls=%async_computation.2 | async-start | bytes 294912 | tf_op jit(solution)/shard_map/all_to_all | solution.py:200
  100.2 0.6 copy-start.4
  100.8 0.6 copy-start.5
  101.4 0.6 copy-start.6
  104.8 9.3 %all-to-all-start.3 = ((bf16[4,128,128]{2,1,0:T(8,128)(2,1)}), bf16[4,128,128]{2,1,0:T(8,128)(2,1)S(1)}, u32[]{:S(2)}, u32[]{:S(2)}) async-start(bf16[4,128,128]{2,1,0:T(8,128)(2,1)} %broadcast_in_dim.14), calls=%async_computation.3 | async-start | bytes 262144 | tf_op jit(solution)/shard_map/all_to_all | solution.py:173
